TPU v7x, 32 devices: a whole 2x2x4 slice. The times are simulated.
32 devices in a mesh: row: 8 (over y, x, core), col: 4 (over z).
Axes of the slice: x: 2, y: 2, z: 4, core: 2. Of those that a mesh axis runs over, the one named last changes fastest.
Arguments:
- activations: bfloat16 [128, 8192], P('row', 'col'), may hold values from -6 to 6
- out_grad: bfloat16 [128, 8192], P('row', 'col'), may hold values from -1.5 to 1.5
- w_gate: bfloat16 [8192, 14336], P('col', 'row'), may hold values from -0.0625 to 0.0625
- w_up: bfloat16 [8192, 14336], P('col', 'row'), may hold values from -0.0625 to 0.0625
- w_down: bfloat16 [14336, 8192], P('row', 'col'), may hold values from -0.046875 to 0.046875
Outputs:
- in_grad: bfloat16 [128, 8192], P('row', 'col')
- grad_gate: bfloat16 [8192, 14336], P('col', 'row')
- grad_up: bfloat16 [8192, 14336], P('col', 'row')
- grad_down: bfloat16 [14336, 8192], P('row', 'col')
All inputs are finite; a program needn't handle non-finite values.
Results may differ from a plain program's by a relative error of at most 0.0049.
Values may be sent and summed in bfloat16 or wider, within the bound.
A program may use at most 128 MiB of HBM per device.

v0:
```python
import jax
import jax.numpy as jnp
from jax import lax
from jax.sharding import PartitionSpec as P


def swiglu_parts(summed, width):
    gate = summed[:, :width]
    up_val = summed[:, width : 2 * width]
    hidden_grad = summed[:, 2 * width :]
    sigma = jax.nn.sigmoid(gate)
    hidden = (gate * sigma * up_val).astype(jnp.bfloat16)
    up_grad = (hidden_grad * gate * sigma).astype(jnp.bfloat16)
    gate_grad = (hidden_grad * up_val * sigma * (1.0 + gate * (1.0 - sigma))).astype(jnp.bfloat16)
    return (hidden, gate_grad, up_grad)


def on_device(activations, out_grad, w_gate, w_up, w_down):
    inputs, grads = (
        lax.all_gather(activations, "row", axis=0, tiled=True),
        lax.all_gather(out_grad, "row", axis=0, tiled=True),
    )
    width = w_gate.shape[1]
    contract_last = (((1,), (1,)), ((), ()))
    contract_first = (((0,), (0,)), ((), ()))
    gate_part = jnp.dot(inputs, w_gate, preferred_element_type=jnp.float32)
    up_part = jnp.dot(inputs, w_up, preferred_element_type=jnp.float32)
    back_part = lax.dot_general(grads, w_down, contract_last, preferred_element_type=jnp.float32)
    summed = lax.psum(jnp.concatenate([gate_part, up_part, back_part], axis=1), "col")
    hidden, gate_grad, up_grad = swiglu_parts(summed, width)
    grad_down = lax.dot_general(
        hidden, grads, contract_first, preferred_element_type=jnp.float32
    ).astype(jnp.bfloat16)
    grad_gate = lax.dot_general(
        inputs, gate_grad, contract_first, preferred_element_type=jnp.float32
    ).astype(jnp.bfloat16)
    grad_up = lax.dot_general(
        inputs, up_grad, contract_first, preferred_element_type=jnp.float32
    ).astype(jnp.bfloat16)
    term = lax.dot_general(gate_grad, w_gate, contract_last, preferred_element_type=jnp.float32)
    in_grad = lax.psum_scatter(
        term + lax.dot_general(up_grad, w_up, contract_last, preferred_element_type=jnp.float32),
        "row",
        scatter_dimension=0,
        tiled=True,
    ).astype(jnp.bfloat16)
    return (in_grad, grad_gate, grad_up, grad_down)


def solution(mesh):
    placed = (P("row", "col"), P("row", "col"), P("col", "row"), P("col", "row"), P("row", "col"))
    return jax.shard_map(
        on_device,
        mesh=mesh,
        in_specs=placed,
        out_specs=(P("row", "col"), P("col", "row"), P("col", "row"), P("row", "col")),
        check_vma=False,
    )
```

profile of v0, /device:TPU:0, one launch (start us, length us, event | category | flops | bytes accessed | tf_op | source)
XLA Modules:
  0.0 204.9 jit_solution(13167971425333426517)
XLA Ops:
  7.2 0.0 all-reduce.2.cloned.1.call-start
  7.2 0.0 slice-start
  7.2 11.9 %all_gather.6 = bf16[128,2048]{1,0:T(8,128)(2,1)S(1)} all-gather(bf16[16,2048]{1,0:T(8,128)(2,1)} %param.5), channel_id=1, replica_groups=mesh['row'=8,'col'=4] {'row'}, dimensions={0}, use_global_device_ids=true | all-gather | bytes 589824 | tf_op jit(solution)/shard_map/all_gather | solution.py:20
  19.1 4.5 %fusion.4 = f32[128,1792]{1,0:T(8,128)S(1)} fusion(bf16[128,2048]{1,0:T(8,128)(2,1)S(1)} %all_gather.6, bf16[2048,1792]{1,0:T(8,128)(2,1)} %param.7), kind=kOutput, calls=%fused_computation.13 | convolution fusion | flops 939524096 | bytes 8781824 | tf_op jit(solution)/shard_map/dot_general | solution.py:26
  23.6 0.0 copy-done
  23.6 0.0 copy-start.8
  23.6 0.0 slice-start.5
  23.6 1.2 fusion.5
  24.8 9.6 %all_gather.7 = bf16[128,2048]{1,0:T(8,128)(2,1)S(1)} all-gather(bf16[16,2048]{1,0:T(8,128)(2,1)S(1)} %copy-done.8), channel_id=1, replica_groups=mesh['row'=8,'col'=4] {'row'}, dimensions={0}, use_global_device_ids=true | all-gather | bytes 589824 | tf_op jit(solution)/shard_map/all_gather | solution.py:21
  34.4 0.0 slice-done.5
  34.4 2.5 %fusion.6 = f32[128,1792]{1,0:T(8,128)S(1)} fusion(bf16[128,2048]{1,0:T(8,128)(2,1)S(1)} %all_gather.7, bf16[1792,2048]{1,0:T(8,128)(2,1)S(1)} %bitcast.24), kind=kOutput, calls=%fused_computation.15 | convolution fusion | flops 939524096 | bytes 8781824 | tf_op jit(solution)/shard_map/dot_general | solution.py:28
  37.0 1.7 pad_maximum_fusion
  38.7 0.0 all-reduce.2.cloned.1.call-update
  38.7 0.2 reduce-scatter.2.cloned.1.call-start
  38.9 108.6 %all-reduce.2.cloned.1.call-done = f32[128,5376]{1,0:T(8,128)} async-done(((f32[128,5376]{1,0:T(8,128)}), f32[128,5376]{1,0:T(8,128)}) %all-reduce.2.cloned.1.call-update) | async-done | bytes 2752528 | tf_op jit(solution)/shard_map/psum | solution.py:29
  147.5 2.1 %multiply_convert_fusion.1 = (bf16[128,1792]{1,0:T(8,128)(2,1)S(1)}, bf16[128,1792]{1,0:T(8,128)(2,1)S(1)}) fusion(f32[128,5376]{1,0:T(8,128)} %all-reduce.2.cloned.1.call-done), kind=kLoop, calls=%fused_computation.8 | loop fusion | flops 2981888 | bytes 3670016 | tf_op jit(solution)/shard_map/convert_element_type | solution.py:13
  149.7 0.0 copy-start.3
  149.7 0.0 copy-start.5
  149.7 0.8 copy-done.3
  150.4 5.7 %fusion.7 = f32[128,2048]{1,0:T(8,128)S(1)} fusion(bf16[128,1792]{1,0:T(8,128)(2,1)S(1)} %get-tuple-element.9, bf16[2048,1792]{1,0:T(8,128)(2,1)} %param.7), kind=kOutput, calls=%fused_computation.16 | convolution fusion | flops 939524096 | bytes 8847360 | tf_op jit(solution)/shard_map/dot_general | solution.py:40
  156.1 0.0 copy-done.5
  156.1 0.0 slice-done.2
  156.2 0.0 slice-done.3
  156.2 3.5 %convolution_add_fusion = f32[128,2048]{1,0:T(8,128)} fusion(f32[128,2048]{1,0:T(8,128)S(1)} %fusion.7, bf16[128,1792]{1,0:T(8,128)(2,1)S(1)} %get-tuple-element.8, bf16[2048,1792]{1,0:T(8,128)(2,1)S(1)} %bitcast.22), kind=kOutput, calls=%fused_computation.6 | convolution fusion | flops 939786240 | bytes 9895936 | tf_op jit(solution)/shard_map/dot_general | solution.py:42
  159.6 0.0 reduce-scatter.2.cloned.1.call-update
  159.7 6.3 %fusion.1 = bf16[2048,1792]{0,1:T(8,128)(2,1)} fusion(bf16[128,1792]{1,0:T(8,128)(2,1)} %copy-done.5, bf16[128,2048]{1,0:T(8,128)(2,1)} %copy-done), kind=kOutput, calls=%fused_computation.4 | convolution fusion | flops 943194112 | bytes 8323072 | tf_op jit(solution)/shard_map/dot_general | solution.py:37
  166.0 10.1 %copy.10 = bf16[2048,1792]{1,0:T(8,128)(2,1)} copy(bf16[2048,1792]{0,1:T(8,128)(2,1)} %fusion.1) | data formatting | bytes 14680064
  176.1 5.1 %fusion = bf16[2048,1792]{0,1:T(8,128)(2,1)} fusion(bf16[128,1792]{1,0:T(8,128)(2,1)S(1)} %copy-done.4, bf16[128,2048]{1,0:T(8,128)(2,1)S(1)} %copy-done.1), kind=kOutput, calls=%fused_computation.3 | convolution fusion | flops 943194112 | bytes 8323072 | tf_op jit(solution)/shard_map/dot_general | solution.py:34
  181.2 10.1 %copy.9 = bf16[2048,1792]{1,0:T(8,128)(2,1)} copy(bf16[2048,1792]{0,1:T(8,128)(2,1)} %fusion) | data formatting | bytes 14680064
  191.3 0.0 copy-done.2
  191.3 5.2 %convolution_convert_fusion = bf16[1792,2048]{1,0:T(8,128)(2,1)} fusion(bf16[128,2048]{1,0:T(8,128)(2,1)S(1)} %copy-done.7, f32[128,5376]{1,0:T(8,128)S(1)} %copy-done.2), kind=kOutput, calls=%fused_computation | convolution fusion | flops 944570368 | bytes 9699328 | tf_op jit(solution)/shard_map/dot_general | solution.py:31
  196.5 1.5 convert_element_type.29
  (22 shorter events, 0.0 us)
Async XLA Ops:
  7.2 140.3 %all-reduce.2.cloned.1.call-start = ((), (), s32[]{:S(2)}) async-start(), calls=%async_computation.1 | async-start | bytes 5505024 | tf_op jit(solution)/shard_map/psum | solution.py:29
  7.2 16.4 %slice-start = ((s8[7340032]{0:T(1024)(128)(4,1)}), s8[4194304]{0:T(1024)(128)(4,1)S(1)}, s32[]{:S(2)}) async-start(s8[7340032]{0:T(1024)(128)(4,1)} %bitcast.19), calls=%async_computation.3 | async-start | bytes 8388608
  19.1 4.5 %copy-start = (bf16[128,2048]{1,0:T(8,128)(2,1)}, bf16[128,2048]{1,0:T(8,128)(2,1)S(1)}, u32[]{:S(2)}) copy-start(bf16[128,2048]{1,0:T(8,128)(2,1)S(1)} %all_gather.6) | copy-start | bytes 1572868
  19.1 4.5 %slice-start.1 = ((s8[7340032]{0:T(1024)(128)(4,1)}), s8[3145728]{0:T(1024)(128)(4,1)S(1)}, s32[]{:S(2)}) async-start(s8[7340032]{0:T(1024)(128)(4,1)} %bitcast.19), calls=%async_computation.4 | async-start | bytes 6291456
  19.1 15.3 %slice-start.4 = ((s8[7340032]{0:T(1024)(128)(4,1)}), s8[4194304]{0:T(1024)(128)(4,1)S(1)}, s32[]{:S(2)}) async-start(s8[7340032]{0:T(1024)(128)(4,1)} %bitcast.23), calls=%async_computation.7 | async-start | bytes 8388608
  23.6 1.2 copy-start.8
  23.6 10.8 %slice-start.5 = ((s8[7340032]{0:T(1024)(128)(4,1)}), s8[3145728]{0:T(1024)(128)(4,1)S(1)}, s32[]{:S(2)}) async-start(s8[7340032]{0:T(1024)(128)(4,1)} %bitcast.23), calls=%async_computation.8 | async-start | bytes 6291456
  34.4 2.6 %copy-start.6 = (bf16[128,2048]{1,0:T(8,128)(2,1)}, bf16[128,2048]{1,0:T(8,128)(2,1)S(1)}, u32[]{:S(2)}) copy-start(bf16[128,2048]{1,0:T(8,128)(2,1)S(1)} %all_gather.7) | copy-start | bytes 1572868
  38.7 117.5 %slice-start.2 = ((s8[7340032]{0:T(1024)(128)(4,1)}), s8[3145728]{0:T(1024)(128)(4,1)S(1)}, s32[]{:S(2)}) async-start(s8[7340032]{0:T(1024)(128)(4,1)} %bitcast.21), calls=%async_computation.5 | async-start | bytes 6291456
  38.7 157.8 %reduce-scatter.2.cloned.1.call-start = ((), (), s32[]{:S(2)}) async-start(), calls=%async_computation.2 | async-start | bytes 1179648 | tf_op jit(solution)/shard_map/reduce_scatter | solution.py:41
  149.7 0.8 copy-start.3
  149.7 6.5 %copy-start.5 = (bf16[128,1792]{1,0:T(8,128)(2,1)}, bf16[128,1792]{1,0:T(8,128)(2,1)S(1)}, u32[]{:S(2)}) copy-start(bf16[128,1792]{1,0:T(8,128)(2,1)S(1)} %get-tuple-element.8) | copy-start | bytes 1376260
  150.4 5.7 %slice-start.3 = ((s8[7340032]{0:T(1024)(128)(4,1)}), s8[4194304]{0:T(1024)(128)(4,1)S(1)}, s32[]{:S(2)}) async-start(s8[7340032]{0:T(1024)(128)(4,1)} %bitcast.21), calls=%async_computation.6 | async-start | bytes 8388608
  166.0 10.1 %copy-start.1 = (bf16[128,2048]{1,0:T(8,128)(2,1)S(1)}, bf16[128,2048]{1,0:T(8,128)(2,1)}, u32[]{:S(2)}) copy-start(bf16[128,2048]{1,0:T(8,128)(2,1)} %copy-done) | copy-start | bytes 1572868
  166.0 10.1 %copy-start.4 = (bf16[128,1792]{1,0:T(8,128)(2,1)S(1)}, bf16[128,1792]{1,0:T(8,128)(2,1)}, u32[]{:S(2)}) copy-start(bf16[128,1792]{1,0:T(8,128)(2,1)} %copy-done.3) | copy-start | bytes 1376260
  181.2 10.1 %copy-start.2 = (f32[128,5376]{1,0:T(8,128)S(1)}, f32[128,5376]{1,0:T(8,128)}, u32[]{:S(2)}) copy-start(f32[128,5376]{1,0:T(8,128)} %all-reduce.2.cloned.1.call-done) | copy-start | bytes 8257540
  181.2 10.1 %copy-start.7 = (bf16[128,2048]{1,0:T(8,128)(2,1)S(1)}, bf16[128,2048]{1,0:T(8,128)(2,1)}, u32[]{:S(2)}) copy-start(bf16[128,2048]{1,0:T(8,128)(2,1)} %copy-done.6) | copy-start | bytes 1572868
Sparse Core Ops, SparseCore 0:
  38.8 108.6 all-reduce.1
  159.8 35.0 reduce-scatter.1
where the time goes:
time: 205 us
  waiting for transfers between devices  109 us (53%)
  matrix products  34 us (17%)
  blocking collectives  21.4 us (10%)
  local copies, waits for them, and re-layouts  21 us (10%)
  between operations  14.2 us (7%)
  other arithmetic  5.4 us (3%)
    psum x1, waiting for transfers between devices, on_device(): lax.psum(jnp.concatenate([gate_part, up_part, back_part], axis=1), 'col')  109 us
    unnamed x32, local copies, waits for them, and re-layouts  21 us
    all_gather x1, blocking collectives, on_device(): lax.all_gather(activations, 'row', axis=0, tiled=True)  11.9 us
    all_gather x1, blocking collectives, on_device(): lax.all_gather(out_grad, 'row', axis=0, tiled=True)  9.55 us
    dot_general x1, matrix products, on_device(): lax.dot_general(inputs, up_grad, contract_first, preferred_element_type=j...  6.32 us
    dot_general x1, matrix products, on_device(): lax.dot_general(gate_grad, w_gate, contract_last, preferred_element_type=...  5.7 us
    dot_general x1, matrix products, on_device(): lax.dot_general(hidden, grads, contract_first, preferred_element_type=jnp...  5.18 us
    dot_general x1, matrix products, on_device(): lax.dot_general(inputs, gate_grad, contract_first, preferred_element_type...  5.15 us
  transfers between devices with their start and end apart: 2, of which 1 were waited for; matrix products, arithmetic and copies ran while one was open for 18% of the time, Pallas kernels for 0%

commit v1 on v0

--- a/solution.py
+++ b/solution.py
@@ -1,6 +1,10 @@
+import functools
+
 import jax
 import jax.numpy as jnp
 from jax import lax
+from jax.experimental import pallas as pl
+from jax.experimental.pallas import tpu as pltpu
 from jax.sharding import PartitionSpec as P
 
 
@@ -47,10 +51,395 @@
     return (in_grad, grad_gate, grad_up, grad_down)
 
 
+MESH = pl.DeviceIdType.MESH
+CHUNK = 256
+
+
+def nt_dot(a, b):
+    return lax.dot_general(a, b, (((1,), (1,)), ((), ())), preferred_element_type=jnp.float32)
+
+
+def tn_dot(a, b):
+    return lax.dot_general(a, b, (((0,), (0,)), ((), ())), preferred_element_type=jnp.float32)
+
+
+def exchange_kernel(
+    act_ref, grad_ref, wg_ref, wu_ref, wd_ref,
+    in_grad_ref, act_out, grad_out, hidden_out, gate_out, up_out,
+    both, wgu, wdn, ep, rp, xp, res, own, acc, pair, send_buf, recv_buf,
+    w_sem, gat_send, gat_recv, ep_send, rp_recv, xp_send, xp_recv, res_send, res_recv,
+    pair_send, pair_recv, rs_send, rs_recv, own_sem,
+):
+    chunks = wgu.shape[0]
+    rows, width = act_ref.shape
+    half = rows * 4
+    r = lax.axis_index("row")
+    c = lax.axis_index("col")
+    core = lax.rem(r, 2)
+    x = lax.rem(r // 2, 2)
+    y = r // 4
+    sib = r + 1 - 2 * core
+    xn = r + 2 - 4 * x
+    yn = r + 4 - 8 * y
+    dg = xn + 4 - 8 * y
+    last = chunks - 1
+
+    def weight_copies(j):
+        cols = pl.ds(pl.multiple_of(j * CHUNK, CHUNK), CHUNK)
+        return (
+            pltpu.make_async_copy(wg_ref.at[:, cols], wgu.at[j, :, pl.ds(0, CHUNK)], w_sem.at[0, j]),
+            pltpu.make_async_copy(wu_ref.at[:, cols], wgu.at[j, :, pl.ds(CHUNK, CHUNK)], w_sem.at[1, j]),
+            pltpu.make_async_copy(wd_ref.at[cols, :], wdn.at[j], w_sem.at[2, j]),
+        )
+
+    def start_weights(j, carry):
+        for copy in weight_copies(j):
+            copy.start()
+        return carry
+
+    barrier = pltpu.get_barrier_semaphore()
+    for other in (sib, xn, yn, dg):
+        pl.semaphore_signal(barrier, inc=1, device_id=(other, c), device_id_type=MESH)
+
+    @pl.when(c > 0)
+    def _():
+        pl.semaphore_signal(barrier, inc=1, device_id=(r, c - 1), device_id_type=MESH)
+
+    @pl.when(c < 3)
+    def _():
+        pl.semaphore_signal(barrier, inc=1, device_id=(r, c + 1), device_id_type=MESH)
+
+    lax.fori_loop(0, chunks, start_weights, 0)
+    mine = pl.ds(pl.multiple_of(r * rows, rows), rows)
+    locals_ = (
+        pltpu.make_async_copy(act_ref, both.at[0, mine], own_sem.at[0]),
+        pltpu.make_async_copy(grad_ref, both.at[1, mine], own_sem.at[1]),
+    )
+    for copy in locals_:
+        copy.start()
+    acc[...] = jnp.zeros_like(acc)
+
+    end = (c == 0) | (c == 3)
+
+    @pl.when(end)
+    def _():
+        pl.semaphore_wait(barrier, 5)
+
+    @pl.when(jnp.logical_not(end))
+    def _():
+        pl.semaphore_wait(barrier, 6)
+
+    def block(a, index):
+        return both.at[a, pl.ds(pl.multiple_of(index * rows, rows), rows)]
+
+    def gather(a, index, to, kind):
+        return pltpu.make_async_remote_copy(
+            src_ref=block(a, index), dst_ref=block(a, index),
+            send_sem=gat_send.at[a, kind], recv_sem=gat_recv.at[a, kind],
+            device_id=(to, c), device_id_type=MESH,
+        )
+
+    for copy in locals_:
+        copy.wait()
+    sent = []
+    for a in (0, 1):
+        sent += [gather(a, r, xn, 0), gather(a, r, yn, 1), gather(a, r, sib, 3)]
+    for copy in sent:
+        copy.start()
+    gather(0, xn, xn, 0).wait_recv()
+    sent.append(gather(0, xn, yn, 2))
+    sent[-1].start()
+    gather(1, yn, yn, 1).wait_recv()
+    sent.append(gather(1, yn, xn, 2))
+    sent[-1].start()
+    for a, index, kind in ((0, xn, 4), (1, yn, 5)):
+        sent.append(gather(a, index, sib, kind))
+        sent[-1].start()
+    gather(0, yn, yn, 1).wait_recv()
+    gather(1, xn, xn, 0).wait_recv()
+    for a, index, kind in ((0, yn, 5), (1, xn, 4)):
+        sent.append(gather(a, index, sib, kind))
+        sent[-1].start()
+    for a in (0, 1):
+        gather(a, dg, yn, 2).wait_recv()
+        sent.append(gather(a, dg, sib, 6))
+        sent[-1].start()
+    for a in (0, 1):
+        for kind, index in ((3, r), (4, xn), (5, yn), (6, dg)):
+            gather(a, index + sib - r, sib, kind).wait_recv()
+
+    act_out[...] = both[0]
+    grad_out[...] = both[1]
+
+    inner = jnp.where(c == 0, 1, 2)
+    outer = jnp.where(c == 1, 0, 3)
+    peer = 3 - c
+    mine_h = jnp.where(c == 2, 1, 0)
+    other_h = 1 - mine_h
+    first_h = jnp.where(c == 0, 1, 0)
+
+    def to_inner(j, h):
+        return pltpu.make_async_remote_copy(
+            src_ref=ep.at[j, h], dst_ref=rp.at[j, h], send_sem=ep_send.at[j, h], recv_sem=rp_recv.at[j, h],
+            device_id=(r, inner), device_id_type=MESH,
+        )
+
+    def from_outer(j, h):
+        return pltpu.make_async_remote_copy(
+            src_ref=ep.at[j, h], dst_ref=rp.at[j, h], send_sem=ep_send.at[j, h], recv_sem=rp_recv.at[j, h],
+            device_id=(r, outer), device_id_type=MESH,
+        )
+
+    def to_peer(j):
+        return pltpu.make_async_remote_copy(
+            src_ref=ep.at[j, other_h], dst_ref=xp.at[j], send_sem=xp_send.at[j], recv_sem=xp_recv.at[j],
+            device_id=(r, peer), device_id_type=MESH,
+        )
+
+    def result(j, h, to, kind):
+        return pltpu.make_async_remote_copy(
+            src_ref=res.at[j, h], dst_ref=res.at[j, h], send_sem=res_send.at[kind, j], recv_sem=res_recv.at[j, h],
+            device_id=(r, to), device_id_type=MESH,
+        )
+
+    def part(j):
+        for copy in weight_copies(j):
+            copy.wait()
+        front = jnp.dot(both[0], wgu[j], preferred_element_type=jnp.float32)
+        back = nt_dot(both[1], wdn[j])
+        return jnp.concatenate([front, back], axis=1)
+
+    def finish(j):
+        cols = pl.ds(pl.multiple_of(j * CHUNK, CHUNK), CHUNK)
+        ready = res[j].reshape(2 * half, 3 * CHUNK)
+        hidden_out[:, cols] = ready[:, :CHUNK]
+        gate_out[:, cols] = ready[:, CHUNK : 2 * CHUNK]
+        up_out[:, cols] = ready[:, 2 * CHUNK :]
+        for n in range(4):
+            span = slice(n * width // 4, (n + 1) * width // 4)
+            acc[:, span] += nt_dot(ready[:, CHUNK:], wgu[j, span, :])
+
+    @pl.when(end)
+    def _():
+        def send(j, carry):
+            total = part(j)
+            ep[j] = total.astype(jnp.bfloat16).reshape(2, half, 3 * CHUNK)
+            to_inner(j, first_h).start()
+            to_inner(j, 1 - first_h).start()
+            return carry
+
+        def take(j, carry):
+            for h in (0, 1):
+                result(j, h, inner, 0).wait_recv()
+            finish(j)
+            return carry
+
+        def drain(j, carry):
+            for h in (0, 1):
+                to_inner(j, h).wait_send()
+            return carry
+
+        lax.fori_loop(0, chunks, send, 0)
+        lax.fori_loop(0, chunks, take, 0)
+        lax.fori_loop(0, chunks, drain, 0)
+
+    @pl.when(jnp.logical_not(end))
+    def _():
+        def step(i, carry):
+            @pl.when(i <= last)
+            def _():
+                own[lax.rem(i, 2)] = part(i).reshape(2, half, 3 * CHUNK)
+                from_outer(i, other_h).wait_recv()
+                ep[i, other_h] = (
+                    own[lax.rem(i, 2), other_h] + rp[i, other_h].astype(jnp.float32)
+                ).astype(jnp.bfloat16)
+                to_peer(i).start()
+
+            @pl.when((i >= 1) & (i <= chunks))
+            def _():
+                j = i - 1
+                from_outer(j, mine_h).wait_recv()
+                to_peer(j).wait_recv()
+                total = own[lax.rem(j, 2), mine_h] + (
+                    rp[j, mine_h].astype(jnp.float32) + xp[j].astype(jnp.float32)
+                )
+                res[j, mine_h] = jnp.concatenate(swiglu_parts(total, CHUNK), axis=1)
+                result(j, mine_h, peer, 0).start()
+                result(j, mine_h, outer, 1).start()
+
+            @pl.when(i >= 2)
+            def _():
+                j = i - 2
+                result(j, other_h, peer, 0).wait_recv()
+                result(j, other_h, outer, 2).start()
+                finish(j)
+
+            return carry
+
+        def drain(j, carry):
+            to_peer(j).wait_send()
+            result(j, mine_h, peer, 0).wait_send()
+            result(j, mine_h, outer, 1).wait_send()
+            result(j, other_h, outer, 2).wait_send()
+            return carry
+
+        lax.fori_loop(0, chunks + 2, step, 0)
+        lax.fori_loop(0, chunks, drain, 0)
+
+    for copy in sent:
+        copy.wait_send()
+
+    def term(index):
+        return pl.ds(pl.multiple_of(index * rows, rows), rows)
+
+    def to_sib(k):
+        return pltpu.make_async_remote_copy(
+            src_ref=acc.at[term(2 * k + 1 - core)], dst_ref=pair.at[k],
+            send_sem=pair_send.at[k], recv_sem=pair_recv.at[k],
+            device_id=(sib, c), device_id_type=MESH,
+        )
+
+    for k in range(4):
+        to_sib(k).start()
+    for k in range(4):
+        to_sib(k).wait_recv()
+
+    def summed(index):
+        return acc[term(index)] + pair[index // 2]
+
+    def to_chip(kind, to):
+        return pltpu.make_async_remote_copy(
+            src_ref=send_buf.at[kind], dst_ref=recv_buf.at[kind],
+            send_sem=rs_send.at[kind], recv_sem=rs_recv.at[kind],
+            device_id=(to, c), device_id_type=MESH,
+        )
+
+    chips = ((2, dg), (0, xn), (1, yn))
+    for kind, to in chips:
+        send_buf[kind] = summed(to).astype(jnp.bfloat16)
+        to_chip(kind, to).start()
+    total = summed(r)
+    for kind, to in chips:
+        to_chip(kind, to).wait_recv()
+        total += recv_buf[kind].astype(jnp.float32)
+    in_grad_ref[...] = total.astype(jnp.bfloat16)
+    for k in range(4):
+        to_sib(k).wait_send()
+    for kind, to in chips:
+        to_chip(kind, to).wait_send()
+
+
+def exchange(activations, out_grad, w_gate, w_up, w_down):
+    rows, width = activations.shape
+    hidden = w_gate.shape[1]
+    tokens, chunks, half = 8 * rows, hidden // CHUNK, 4 * rows
+    vmem = pl.BlockSpec(memory_space=pltpu.VMEM)
+    anywhere = pl.BlockSpec(memory_space=pl.ANY)
+    bf16, f32, dma = jnp.bfloat16, jnp.float32, pltpu.SemaphoreType.DMA
+    return pl.pallas_call(
+        exchange_kernel,
+        out_shape=(
+            jax.ShapeDtypeStruct((rows, width), bf16),
+            jax.ShapeDtypeStruct((tokens, width), bf16),
+            jax.ShapeDtypeStruct((tokens, width), bf16),
+            jax.ShapeDtypeStruct((tokens, hidden), bf16),
+            jax.ShapeDtypeStruct((tokens, hidden), bf16),
+            jax.ShapeDtypeStruct((tokens, hidden), bf16),
+        ),
+        in_specs=[vmem, vmem, anywhere, anywhere, anywhere],
+        out_specs=(vmem,) * 6,
+        scratch_shapes=[
+            pltpu.VMEM((2, tokens, width), bf16),
+            pltpu.VMEM((chunks, width, 2 * CHUNK), bf16),
+            pltpu.VMEM((chunks, CHUNK, width), bf16),
+            pltpu.VMEM((chunks, 2, half, 3 * CHUNK), bf16),
+            pltpu.VMEM((chunks, 2, half, 3 * CHUNK), bf16),
+            pltpu.VMEM((chunks, half, 3 * CHUNK), bf16),
+            pltpu.VMEM((chunks, 2, half, 3 * CHUNK), bf16),
+            pltpu.VMEM((2, 2, half, 3 * CHUNK), f32),
+            pltpu.VMEM((tokens, width), f32),
+            pltpu.VMEM((4, rows, width), f32),
+            pltpu.VMEM((3, rows, width), bf16),
+            pltpu.VMEM((3, rows, width), bf16),
+            dma((3, chunks)), dma((2, 7)), dma((2, 7)),
+            dma((chunks, 2)), dma((chunks, 2)), dma((chunks,)), dma((chunks,)),
+            dma((3, chunks)), dma((chunks, 2)),
+            dma((4,)), dma((4,)), dma((3,)), dma((3,)), dma((2,)),
+        ],
+        compiler_params=pltpu.CompilerParams(
+            collective_id=0, has_side_effects=True, vmem_limit_bytes=56 * 1024 * 1024
+        ),
+        cost_estimate=pl.CostEstimate(
+            flops=10 * tokens * width * hidden,
+            bytes_accessed=6 * width * hidden,
+            transcendentals=tokens * hidden,
+        ),
+    )(activations, out_grad, w_gate, w_up, w_down)
+
+
+def outer_kernel(split, act_ref, grad_ref, hidden_ref, gate_ref, up_ref, gate_out, up_out, down_out):
+    i = pl.program_id(0)
+
+    @pl.when(i < split)
+    def _():
+        gate_out[...] = tn_dot(act_ref[...], gate_ref[...]).astype(jnp.bfloat16)
+        up_out[...] = tn_dot(act_ref[...], up_ref[...]).astype(jnp.bfloat16)
+
+    @pl.when(i >= split)
+    def _():
+        down_out[...] = tn_dot(hidden_ref[...], grad_ref[...]).astype(jnp.bfloat16)
+
+
+def outer_products(act, grad, hidden, gate_grad, up_grad):
+    tokens, width = act.shape
+    units = hidden.shape[1]
+    tile = 256
+    split = width // tile
+    early = lambda i: jnp.minimum(i, split - 1)
+    late = lambda i: jnp.maximum(i - split, 0)
+    whole = lambda i: (0, 0)
+    return pl.pallas_call(
+        functools.partial(outer_kernel, split),
+        grid=(split + units // tile,),
+        out_shape=(
+            jax.ShapeDtypeStruct((width, units), jnp.bfloat16),
+            jax.ShapeDtypeStruct((width, units), jnp.bfloat16),
+            jax.ShapeDtypeStruct((units, width), jnp.bfloat16),
+        ),
+        in_specs=[
+            pl.BlockSpec((tokens, tile), lambda i: (0, early(i))),
+            pl.BlockSpec((tokens, width), whole),
+            pl.BlockSpec((tokens, tile), lambda i: (0, late(i))),
+            pl.BlockSpec((tokens, units), whole),
+            pl.BlockSpec((tokens, units), whole),
+        ],
+        out_specs=(
+            pl.BlockSpec((tile, units), lambda i: (early(i), 0)),
+            pl.BlockSpec((tile, units), lambda i: (early(i), 0)),
+            pl.BlockSpec((tile, width), lambda i: (late(i), 0)),
+        ),
+        compiler_params=pltpu.CompilerParams(vmem_limit_bytes=40 * 1024 * 1024),
+        cost_estimate=pl.CostEstimate(
+            flops=6 * tokens * width * units,
+            bytes_accessed=6 * width * units,
+            transcendentals=0,
+        ),
+    )(act, grad, hidden, gate_grad, up_grad)
+
+
+def on_device_fused(activations, out_grad, w_gate, w_up, w_down):
+    in_grad, act, grad, hidden, gate_grad, up_grad = exchange(
+        activations, out_grad, w_gate, w_up, w_down
+    )
+    grad_gate, grad_up, grad_down = outer_products(act, grad, hidden, gate_grad, up_grad)
+    return (in_grad, grad_gate, grad_up, grad_down)
+
+
 def solution(mesh):
     placed = (P("row", "col"), P("row", "col"), P("col", "row"), P("col", "row"), P("row", "col"))
+    fused = mesh.axis_names == ("row", "col") and dict(mesh.shape) == {"row": 8, "col": 4}
     return jax.shard_map(
-        on_device,
+        on_device_fused if fused else on_device,
         mesh=mesh,
         in_specs=placed,
         out_specs=(P("row", "col"), P("col", "row"), P("col", "row"), P("row", "col")),

time: 205 us -> 88.4 us (0.43)
  waiting for transfers between devices: 109 us -> 0 us
  Pallas kernels: 0 us -> 81.6 us
  matrix products: 34 us -> 0 us
  blocking collectives: 21.4 us -> 0 us
  local copies, waits for them, and re-layouts: 21 us -> 5.76 us
  between operations: 14.2 us -> 0.65 us
  other arithmetic: 5.4 us -> 0 us
    psum x1 -> x0, waiting for transfers between devices: 109 us -> none  [on_device(): lax.psum(jnp.concatenate([gate_part, up_part, back_part], axis=1), 'col')]
    pallas_call x0 -> x2, Pallas kernels: none -> 81.6 us  [the longest x1 67.8 us: exchange(): pl.pallas_call(exchange_kernel, out_shape=(jax.ShapeDtypeStruct((rows, wi...]
    dot_general x8 -> x0, matrix products: 34 us -> none  [the longest x1 6.32 us: on_device(): lax.dot_general(inputs, up_grad, contract_first, preferred_element_type=j...]
    all_gather x2 -> x0, blocking collectives: 21.4 us -> none  [the longest x1 11.9 us: on_device(): lax.all_gather(activations, 'row', axis=0, tiled=True)]
    unnamed x32 -> x13, local copies, waits for them, and re-layouts: 21 us -> 5.76 us
    convert_element_type x2 -> x0, other arithmetic: 3.69 us -> none  [the longest x1 2.15 us: swiglu_parts(): up_grad = (hidden_grad * gate * sigma).astype(jnp.bfloat16)]
  transfers between devices with their start and end apart: 2 -> 0, of which waited for: 1 -> 0; matrix products, arithmetic and copies ran while one was open for 18% -> 0% of each run, Pallas kernels for 0% -> 0%
where the time goes in v1:
time: 88.4 us; the launch traced here: 88.1 us
  Pallas kernels  81.6 us (92%)
  local copies, waits for them, and re-layouts  5.76 us (7%)
    pallas_call x1, Pallas kernels, exchange(): pl.pallas_call(exchange_kernel, out_shape=(jax.ShapeDtypeStruct((rows, wi...  67.8 us
    pallas_call x1, Pallas kernels, outer_products(): pl.pallas_call(functools.partial(outer_kernel, split), grid=(split + unit...  13.9 us
    unnamed x13, local copies, waits for them, and re-layouts  5.76 us

profile of v1, /device:TPU:0, one launch (start us, length us, event | category | flops | bytes accessed | tf_op | source)
XLA Modules:
  0.0 88.1 jit_solution(949743710860993279)
XLA Ops:
  0.6 67.8 %shard_map.84 = (bf16[16,2048]{1,0:T(8,128)(2,1)}, bf16[128,2048]{1,0:T(8,128)(2,1)}, bf16[128,2048]{1,0:T(8,128)(2,1)}, bf16[128,1792]{1,0:T(8,128)(2,1)}, bf16...) custom-call(bf16[16,2048]{1,0:T(8,128)(2,1)} %act_ref.1, bf16[16,2048]{1,0:T(8,128)(2,1)} %grad_ref.1, ...), custom_call_target="tpu_custom_call" | custom-call | flops 4697620480 | bytes 22020096 | tf_op jit(solution)/shard_map/pallas_call | solution.py:339
  68.4 0.0 copy-start
  68.4 1.0 %copy-done = bf16[128,2048]{1,0:T(8,128)(2,1)S(1)} copy-done((bf16[128,2048]{1,0:T(8,128)(2,1)S(1)}, bf16[128,2048]{1,0:T(8,128)(2,1)}, u32[]{:S(2)}) %copy-start) | copy-done | bytes 524312
  69.5 0.0 copy-start.1
  69.5 1.0 %copy-done.1 = bf16[128,2048]{1,0:T(8,128)(2,1)S(1)} copy-done((bf16[128,2048]{1,0:T(8,128)(2,1)S(1)}, bf16[128,2048]{1,0:T(8,128)(2,1)}, u32[]{:S(2)}) %copy-start.1) | copy-done | bytes 524312
  70.5 0.0 copy-start.2
  70.5 1.0 %copy-done.2 = bf16[128,1792]{1,0:T(8,128)(2,1)S(1)} copy-done((bf16[128,1792]{1,0:T(8,128)(2,1)S(1)}, bf16[128,1792]{1,0:T(8,128)(2,1)}, u32[]{:S(2)}) %copy-start.2) | copy-done | bytes 458776
  71.5 0.0 copy-start.3
  71.5 1.0 %copy-done.3 = bf16[128,1792]{1,0:T(8,128)(2,1)S(1)} copy-done((bf16[128,1792]{1,0:T(8,128)(2,1)S(1)}, bf16[128,1792]{1,0:T(8,128)(2,1)}, u32[]{:S(2)}) %copy-start.3) | copy-done | bytes 458776
  72.5 0.0 copy-start.4
  72.5 1.0 %copy-done.4 = bf16[128,1792]{1,0:T(8,128)(2,1)S(1)} copy-done((bf16[128,1792]{1,0:T(8,128)(2,1)S(1)}, bf16[128,1792]{1,0:T(8,128)(2,1)}, u32[]{:S(2)}) %copy-start.4) | copy-done | bytes 458776
  73.6 0.0 copy-start.5
  73.6 13.9 %shard_map.85 = (bf16[2048,1792]{1,0:T(8,128)(2,1)}, bf16[2048,1792]{1,0:T(8,128)(2,1)}, bf16[1792,2048]{1,0:T(8,128)(2,1)}) custom-call(bf16[128,2048]{1,0:T(8,128)(2,1)S(1)} %copy-done, bf16[128,2048]{1,0:T(8,128)(2,1)S(1)} %copy-done.1, bf16[128,1792]{1,0:T(8,128)(2,1)S(1)} %copy-done.2, bf16[128,1792]{1,0:T(8,128)(2,1)S(1)} %copy-done.3, ...), custom_call_target="tpu_custom_call" | custom-call | flops 2818572288 | bytes 22020096 | tf_op jit(solution)/shard_map/pallas_call | solution.py:401
  87.4 0.0 copy-done.5
  87.4 0.6 copy.10
Async XLA Ops:
  68.4 1.0 %copy-start = (bf16[128,2048]{1,0:T(8,128)(2,1)S(1)}, bf16[128,2048]{1,0:T(8,128)(2,1)}, u32[]{:S(2)}) copy-start(bf16[128,2048]{1,0:T(8,128)(2,1)} %get-tuple-element.14.act_ref) | copy-start | bytes 1572868
  69.5 1.0 %copy-start.1 = (bf16[128,2048]{1,0:T(8,128)(2,1)S(1)}, bf16[128,2048]{1,0:T(8,128)(2,1)}, u32[]{:S(2)}) copy-start(bf16[128,2048]{1,0:T(8,128)(2,1)} %get-tuple-element.15.grad_ref) | copy-start | bytes 1572868
  70.5 1.0 %copy-start.2 = (bf16[128,1792]{1,0:T(8,128)(2,1)S(1)}, bf16[128,1792]{1,0:T(8,128)(2,1)}, u32[]{:S(2)}) copy-start(bf16[128,1792]{1,0:T(8,128)(2,1)} %get-tuple-element.16.hidden_ref) | copy-start | bytes 1376260
  71.5 1.0 %copy-start.3 = (bf16[128,1792]{1,0:T(8,128)(2,1)S(1)}, bf16[128,1792]{1,0:T(8,128)(2,1)}, u32[]{:S(2)}) copy-start(bf16[128,1792]{1,0:T(8,128)(2,1)} %get-tuple-element.17.gate_ref) | copy-start | bytes 1376260
  72.5 1.0 %copy-start.4 = (bf16[128,1792]{1,0:T(8,128)(2,1)S(1)}, bf16[128,1792]{1,0:T(8,128)(2,1)}, u32[]{:S(2)}) copy-start(bf16[128,1792]{1,0:T(8,128)(2,1)} %get-tuple-element.18.up_ref) | copy-start | bytes 1376260
  73.6 13.9 %copy-start.5 = (bf16[16,2048]{1,0:T(8,128)(2,1)S(1)}, bf16[16,2048]{1,0:T(8,128)(2,1)}, u32[]{:S(2)}) copy-start(bf16[16,2048]{1,0:T(8,128)(2,1)} %get-tuple-element.26) | copy-start | bytes 196612

commit v2 on v1

--- a/solution.py
+++ b/solution.py
@@ -52,21 +52,13 @@
 
 
 MESH = pl.DeviceIdType.MESH
-CHUNK = 256
-
-
-def nt_dot(a, b):
-    return lax.dot_general(a, b, (((1,), (1,)), ((), ())), preferred_element_type=jnp.float32)
-
-
-def tn_dot(a, b):
-    return lax.dot_general(a, b, (((0,), (0,)), ((), ())), preferred_element_type=jnp.float32)
+CHUNK = 128
 
 
 def exchange_kernel(
     act_ref, grad_ref, wg_ref, wu_ref, wd_ref,
-    in_grad_ref, act_out, grad_out, hidden_out, gate_out, up_out,
-    both, wgu, wdn, ep, rp, xp, res, own, acc, pair, send_buf, recv_buf,
+    in_grad_ref, act_t_out, grad_out, hidden_t_out, gate_out, up_out,
+    both, grad_t, wgu, wdn, ep, rp, xp, res, own, acc_t, acc, pair, send_buf, recv_buf,
     w_sem, gat_send, gat_recv, ep_send, rp_recv, xp_send, xp_recv, res_send, res_recv,
     pair_send, pair_recv, rs_send, rs_recv, own_sem,
 ):
@@ -117,7 +109,7 @@
     )
     for copy in locals_:
         copy.start()
-    acc[...] = jnp.zeros_like(acc)
+    acc_t[...] = jnp.zeros_like(acc_t)
 
     end = (c == 0) | (c == 3)
 
@@ -168,8 +160,7 @@
         for kind, index in ((3, r), (4, xn), (5, yn), (6, dg)):
             gather(a, index + sib - r, sib, kind).wait_recv()
 
-    act_out[...] = both[0]
-    grad_out[...] = both[1]
+    grad_t[...] = both[1].T
 
     inner = jnp.where(c == 0, 1, 2)
     outer = jnp.where(c == 1, 0, 3)
@@ -206,18 +197,25 @@
         for copy in weight_copies(j):
             copy.wait()
         front = jnp.dot(both[0], wgu[j], preferred_element_type=jnp.float32)
-        back = nt_dot(both[1], wdn[j])
-        return jnp.concatenate([front, back], axis=1)
+        back = jnp.dot(wdn[j], grad_t[...], preferred_element_type=jnp.float32)
+        return jnp.concatenate([front, back.T], axis=1)
 
     def finish(j):
         cols = pl.ds(pl.multiple_of(j * CHUNK, CHUNK), CHUNK)
         ready = res[j].reshape(2 * half, 3 * CHUNK)
-        hidden_out[:, cols] = ready[:, :CHUNK]
+        hidden_t_out[cols, :] = ready[:, :CHUNK].T
         gate_out[:, cols] = ready[:, CHUNK : 2 * CHUNK]
         up_out[:, cols] = ready[:, 2 * CHUNK :]
+        both_t = ready[:, CHUNK:].T
         for n in range(4):
             span = slice(n * width // 4, (n + 1) * width // 4)
-            acc[:, span] += nt_dot(ready[:, CHUNK:], wgu[j, span, :])
+            acc_t[span, :] += jnp.dot(wgu[j, span, :], both_t, preferred_element_type=jnp.float32)
+
+        @pl.when(j < 8)
+        def _():
+            span = pl.ds(pl.multiple_of(j * (width // 8), width // 8), width // 8)
+            act_t_out[span, :] = both[0, :, span].T
+            grad_out[:, span] = both[1, :, span]
 
     @pl.when(end)
     def _():
@@ -288,6 +286,8 @@
 
     for copy in sent:
         copy.wait_send()
+
+    acc[...] = acc_t[...].T
 
     def term(index):
         return pl.ds(pl.multiple_of(index * rows, rows), rows)
@@ -340,9 +340,9 @@
         exchange_kernel,
         out_shape=(
             jax.ShapeDtypeStruct((rows, width), bf16),
+            jax.ShapeDtypeStruct((width, tokens), bf16),
             jax.ShapeDtypeStruct((tokens, width), bf16),
-            jax.ShapeDtypeStruct((tokens, width), bf16),
-            jax.ShapeDtypeStruct((tokens, hidden), bf16),
+            jax.ShapeDtypeStruct((hidden, tokens), bf16),
             jax.ShapeDtypeStruct((tokens, hidden), bf16),
             jax.ShapeDtypeStruct((tokens, hidden), bf16),
         ),
@@ -350,6 +350,7 @@
         out_specs=(vmem,) * 6,
         scratch_shapes=[
             pltpu.VMEM((2, tokens, width), bf16),
+            pltpu.VMEM((width, tokens), bf16),
             pltpu.VMEM((chunks, width, 2 * CHUNK), bf16),
             pltpu.VMEM((chunks, CHUNK, width), bf16),
             pltpu.VMEM((chunks, 2, half, 3 * CHUNK), bf16),
@@ -357,6 +358,7 @@
             pltpu.VMEM((chunks, half, 3 * CHUNK), bf16),
             pltpu.VMEM((chunks, 2, half, 3 * CHUNK), bf16),
             pltpu.VMEM((2, 2, half, 3 * CHUNK), f32),
+            pltpu.VMEM((width, tokens), f32),
             pltpu.VMEM((tokens, width), f32),
             pltpu.VMEM((4, rows, width), f32),
             pltpu.VMEM((3, rows, width), bf16),
@@ -377,61 +379,60 @@
     )(activations, out_grad, w_gate, w_up, w_down)
 
 
-def outer_kernel(split, act_ref, grad_ref, hidden_ref, gate_ref, up_ref, gate_out, up_out, down_out):
-    i = pl.program_id(0)
-
-    @pl.when(i < split)
-    def _():
-        gate_out[...] = tn_dot(act_ref[...], gate_ref[...]).astype(jnp.bfloat16)
-        up_out[...] = tn_dot(act_ref[...], up_ref[...]).astype(jnp.bfloat16)
-
-    @pl.when(i >= split)
-    def _():
-        down_out[...] = tn_dot(hidden_ref[...], grad_ref[...]).astype(jnp.bfloat16)
-
-
-def outer_products(act, grad, hidden, gate_grad, up_grad):
-    tokens, width = act.shape
-    units = hidden.shape[1]
+def outer_kernel(act_t_ref, grad_ref, hidden_t_ref, gate_ref, up_ref, gate_out, up_out, down_out):
     tile = 256
-    split = width // tile
-    early = lambda i: jnp.minimum(i, split - 1)
-    late = lambda i: jnp.maximum(i - split, 0)
+    for left, right, out in (
+        (act_t_ref, gate_ref, gate_out),
+        (act_t_ref, up_ref, up_out),
+        (hidden_t_ref, grad_ref, down_out),
+    ):
+        for n in range(out.shape[1] // tile):
+            span = slice(n * tile, (n + 1) * tile)
+            out[:, span] = jnp.dot(
+                left[...], right[:, span], preferred_element_type=jnp.float32
+            ).astype(jnp.bfloat16)
+
+
+def outer_products(act_t, grad, hidden_t, gate_grad, up_grad):
+    width, tokens = act_t.shape
+    units = hidden_t.shape[0]
+    steps = 8
+    down = lambda i: (i, 0)
     whole = lambda i: (0, 0)
     return pl.pallas_call(
-        functools.partial(outer_kernel, split),
-        grid=(split + units // tile,),
+        outer_kernel,
+        grid=(steps,),
         out_shape=(
             jax.ShapeDtypeStruct((width, units), jnp.bfloat16),
             jax.ShapeDtypeStruct((width, units), jnp.bfloat16),
             jax.ShapeDtypeStruct((units, width), jnp.bfloat16),
         ),
         in_specs=[
-            pl.BlockSpec((tokens, tile), lambda i: (0, early(i))),
+            pl.BlockSpec((width // steps, tokens), down),
             pl.BlockSpec((tokens, width), whole),
-            pl.BlockSpec((tokens, tile), lambda i: (0, late(i))),
+            pl.BlockSpec((units // steps, tokens), down),
             pl.BlockSpec((tokens, units), whole),
             pl.BlockSpec((tokens, units), whole),
         ],
         out_specs=(
-            pl.BlockSpec((tile, units), lambda i: (early(i), 0)),
-            pl.BlockSpec((tile, units), lambda i: (early(i), 0)),
-            pl.BlockSpec((tile, width), lambda i: (late(i), 0)),
-        ),
-        compiler_params=pltpu.CompilerParams(vmem_limit_bytes=40 * 1024 * 1024),
+            pl.BlockSpec((width // steps, units), down),
+            pl.BlockSpec((width // steps, units), down),
+            pl.BlockSpec((units // steps, width), down),
+        ),
+        compiler_params=pltpu.CompilerParams(vmem_limit_bytes=60 * 1024 * 1024),
         cost_estimate=pl.CostEstimate(
             flops=6 * tokens * width * units,
             bytes_accessed=6 * width * units,
             transcendentals=0,
         ),
-    )(act, grad, hidden, gate_grad, up_grad)
+    )(act_t, grad, hidden_t, gate_grad, up_grad)
 
 
 def on_device_fused(activations, out_grad, w_gate, w_up, w_down):
-    in_grad, act, grad, hidden, gate_grad, up_grad = exchange(
+    in_grad, act_t, grad, hidden_t, gate_grad, up_grad = exchange(
         activations, out_grad, w_gate, w_up, w_down
     )
-    grad_gate, grad_up, grad_down = outer_products(act, grad, hidden, gate_grad, up_grad)
+    grad_gate, grad_up, grad_down = outer_products(act_t, grad, hidden_t, gate_grad, up_grad)
     return (in_grad, grad_gate, grad_up, grad_down)
 
 

time: 88.4 us -> 83 us (0.939)
  local copies, waits for them, and re-layouts: 5.76 us -> 0.63 us
  Pallas kernels: 81.6 us -> 80.5 us
    unnamed x13 -> x3, local copies, waits for them, and re-layouts: 5.76 us -> 0.63 us
    pallas_call x1, Pallas kernels: 13.9 us -> 10.3 us  [outer_products(): pl.pallas_call(outer_kernel, grid=(steps,), out_shape=(jax.ShapeDtypeStru...]
    pallas_call x1, Pallas kernels: 67.8 us -> 70.2 us  [exchange(): pl.pallas_call(exchange_kernel, out_shape=(jax.ShapeDtypeStruct((rows, wi...]
where the time goes in v2:
time: 83 us; the launch traced here: 81.8 us
  Pallas kernels  80.5 us (97%)
    pallas_call x1, Pallas kernels, exchange(): pl.pallas_call(exchange_kernel, out_shape=(jax.ShapeDtypeStruct((rows, wi...  70.2 us
    pallas_call x1, Pallas kernels, outer_products(): pl.pallas_call(outer_kernel, grid=(steps,), out_shape=(jax.ShapeDtypeStru...  10.3 us

profile of v2, /device:TPU:0, one launch (start us, length us, event | category | flops | bytes accessed | tf_op | source)
XLA Modules:
  0.0 81.8 jit_solution(1941492366835434126)
XLA Ops:
  0.6 70.2 %shard_map.84 = (bf16[16,2048]{1,0:T(8,128)(2,1)}, bf16[2048,128]{1,0:T(8,128)(2,1)}, bf16[128,2048]{1,0:T(8,128)(2,1)}, bf16[1792,128]{1,0:T(8,128)(2,1)}, bf16...) custom-call(bf16[16,2048]{1,0:T(8,128)(2,1)} %act_ref.1, bf16[16,2048]{1,0:T(8,128)(2,1)} %grad_ref.1, ...), custom_call_target="tpu_custom_call" | custom-call | flops 4697620480 | bytes 22020096 | tf_op jit(solution)/shard_map/pallas_call | solution.py:339
  70.9 0.0 copy-start
  70.9 10.3 %shard_map.85 = (bf16[2048,1792]{1,0:T(8,128)(2,1)}, bf16[2048,1792]{1,0:T(8,128)(2,1)}, bf16[1792,2048]{1,0:T(8,128)(2,1)}) custom-call(bf16[2048,128]{1,0:T(8,128)(2,1)} %get-tuple-element.14.act_t_ref, bf16[128,2048]{1,0:T(8,128)(2,1)} %get-tuple-element.15.grad_ref, bf16[1792,128]{1,0:T(8,128)(2,1)} %get-tuple-element.16.hidden_t_ref, ...), custom_call_target="tpu_custom_call" | custom-call | flops 2818572288 | bytes 22020096 | tf_op jit(solution)/shard_map/pallas_call | solution.py:402
  81.2 0.0 copy-done
  81.2 0.6 copy.10
Async XLA Ops:
  70.9 10.3 %copy-start = (bf16[16,2048]{1,0:T(8,128)(2,1)S(1)}, bf16[16,2048]{1,0:T(8,128)(2,1)}, u32[]{:S(2)}) copy-start(bf16[16,2048]{1,0:T(8,128)(2,1)} %get-tuple-element.26) | copy-start | bytes 196612

commit v3 on v2

--- a/solution.py
+++ b/solution.py
@@ -53,15 +53,25 @@
 
 MESH = pl.DeviceIdType.MESH
 CHUNK = 128
+ADD_LAG, PASS_LAG = 2, 4
+
+
+def nt_dot(a, b):
+    return lax.dot_general(a, b, (((1,), (1,)), ((), ())), preferred_element_type=jnp.float32)
+
+
+def tn_dot(a, b):
+    return lax.dot_general(a, b, (((0,), (0,)), ((), ())), preferred_element_type=jnp.float32)
 
 
 def exchange_kernel(
     act_ref, grad_ref, wg_ref, wu_ref, wd_ref,
-    in_grad_ref, act_t_out, grad_out, hidden_t_out, gate_out, up_out,
-    both, grad_t, wgu, wdn, ep, rp, xp, res, own, acc_t, acc, pair, send_buf, recv_buf,
+    mine_ref, x_ref, y_ref, diag_ref, act_t_out, grad_out, hidden_t_out, gate_out, up_out,
+    both, wgu, wdn, ep, rp, xp, res, own, acc, pair,
     w_sem, gat_send, gat_recv, ep_send, rp_recv, xp_send, xp_recv, res_send, res_recv,
-    pair_send, pair_recv, rs_send, rs_recv, own_sem,
+    pair_send, pair_recv, own_sem,
 ):
+    chip_refs = (x_ref, y_ref, diag_ref)
     chunks = wgu.shape[0]
     rows, width = act_ref.shape
     half = rows * 4
@@ -109,7 +119,7 @@
     )
     for copy in locals_:
         copy.start()
-    acc_t[...] = jnp.zeros_like(acc_t)
+    acc[...] = jnp.zeros_like(acc)
 
     end = (c == 0) | (c == 3)
 
@@ -160,8 +170,6 @@
         for kind, index in ((3, r), (4, xn), (5, yn), (6, dg)):
             gather(a, index + sib - r, sib, kind).wait_recv()
 
-    grad_t[...] = both[1].T
-
     inner = jnp.where(c == 0, 1, 2)
     outer = jnp.where(c == 1, 0, 3)
     peer = 3 - c
@@ -197,8 +205,8 @@
         for copy in weight_copies(j):
             copy.wait()
         front = jnp.dot(both[0], wgu[j], preferred_element_type=jnp.float32)
-        back = jnp.dot(wdn[j], grad_t[...], preferred_element_type=jnp.float32)
-        return jnp.concatenate([front, back.T], axis=1)
+        back = nt_dot(both[1], wdn[j])
+        return jnp.concatenate([front, back], axis=1)
 
     def finish(j):
         cols = pl.ds(pl.multiple_of(j * CHUNK, CHUNK), CHUNK)
@@ -206,10 +214,9 @@
         hidden_t_out[cols, :] = ready[:, :CHUNK].T
         gate_out[:, cols] = ready[:, CHUNK : 2 * CHUNK]
         up_out[:, cols] = ready[:, 2 * CHUNK :]
-        both_t = ready[:, CHUNK:].T
         for n in range(4):
             span = slice(n * width // 4, (n + 1) * width // 4)
-            acc_t[span, :] += jnp.dot(wgu[j, span, :], both_t, preferred_element_type=jnp.float32)
+            acc[:, span] += nt_dot(ready[:, CHUNK:], wgu[j, span, :])
 
         @pl.when(j < 8)
         def _():
@@ -246,28 +253,28 @@
         def step(i, carry):
             @pl.when(i <= last)
             def _():
-                own[lax.rem(i, 2)] = part(i).reshape(2, half, 3 * CHUNK)
+                own[lax.rem(i, 4)] = part(i).reshape(2, half, 3 * CHUNK)
                 from_outer(i, other_h).wait_recv()
                 ep[i, other_h] = (
-                    own[lax.rem(i, 2), other_h] + rp[i, other_h].astype(jnp.float32)
+                    own[lax.rem(i, 4), other_h] + rp[i, other_h].astype(jnp.float32)
                 ).astype(jnp.bfloat16)
                 to_peer(i).start()
 
-            @pl.when((i >= 1) & (i <= chunks))
+            @pl.when((i >= ADD_LAG) & (i < chunks + ADD_LAG))
             def _():
-                j = i - 1
+                j = i - ADD_LAG
                 from_outer(j, mine_h).wait_recv()
                 to_peer(j).wait_recv()
-                total = own[lax.rem(j, 2), mine_h] + (
+                total = own[lax.rem(j, 4), mine_h] + (
                     rp[j, mine_h].astype(jnp.float32) + xp[j].astype(jnp.float32)
                 )
                 res[j, mine_h] = jnp.concatenate(swiglu_parts(total, CHUNK), axis=1)
                 result(j, mine_h, peer, 0).start()
                 result(j, mine_h, outer, 1).start()
 
-            @pl.when(i >= 2)
+            @pl.when(i >= PASS_LAG)
             def _():
-                j = i - 2
+                j = i - PASS_LAG
                 result(j, other_h, peer, 0).wait_recv()
                 result(j, other_h, outer, 2).start()
                 finish(j)
@@ -281,13 +288,11 @@
             result(j, other_h, outer, 2).wait_send()
             return carry
 
-        lax.fori_loop(0, chunks + 2, step, 0)
+        lax.fori_loop(0, chunks + PASS_LAG, step, 0)
         lax.fori_loop(0, chunks, drain, 0)
 
     for copy in sent:
         copy.wait_send()
-
-    acc[...] = acc_t[...].T
 
     def term(index):
         return pl.ds(pl.multiple_of(index * rows, rows), rows)
@@ -307,26 +312,11 @@
     def summed(index):
         return acc[term(index)] + pair[index // 2]
 
-    def to_chip(kind, to):
-        return pltpu.make_async_remote_copy(
-            src_ref=send_buf.at[kind], dst_ref=recv_buf.at[kind],
-            send_sem=rs_send.at[kind], recv_sem=rs_recv.at[kind],
-            device_id=(to, c), device_id_type=MESH,
-        )
-
-    chips = ((2, dg), (0, xn), (1, yn))
-    for kind, to in chips:
-        send_buf[kind] = summed(to).astype(jnp.bfloat16)
-        to_chip(kind, to).start()
-    total = summed(r)
-    for kind, to in chips:
-        to_chip(kind, to).wait_recv()
-        total += recv_buf[kind].astype(jnp.float32)
-    in_grad_ref[...] = total.astype(jnp.bfloat16)
+    mine_ref[...] = summed(r)
+    for kind, to in enumerate((xn, yn, dg)):
+        chip_refs[kind][...] = summed(to).astype(jnp.bfloat16)
     for k in range(4):
         to_sib(k).wait_send()
-    for kind, to in chips:
-        to_chip(kind, to).wait_send()
 
 
 def exchange(activations, out_grad, w_gate, w_up, w_down):
@@ -339,6 +329,9 @@
     return pl.pallas_call(
         exchange_kernel,
         out_shape=(
+            jax.ShapeDtypeStruct((rows, width), f32),
+            jax.ShapeDtypeStruct((rows, width), bf16),
+            jax.ShapeDtypeStruct((rows, width), bf16),
             jax.ShapeDtypeStruct((rows, width), bf16),
             jax.ShapeDtypeStruct((width, tokens), bf16),
             jax.ShapeDtypeStruct((tokens, width), bf16),
@@ -347,26 +340,22 @@
             jax.ShapeDtypeStruct((tokens, hidden), bf16),
         ),
         in_specs=[vmem, vmem, anywhere, anywhere, anywhere],
-        out_specs=(vmem,) * 6,
+        out_specs=(vmem,) * 9,
         scratch_shapes=[
             pltpu.VMEM((2, tokens, width), bf16),
-            pltpu.VMEM((width, tokens), bf16),
             pltpu.VMEM((chunks, width, 2 * CHUNK), bf16),
             pltpu.VMEM((chunks, CHUNK, width), bf16),
             pltpu.VMEM((chunks, 2, half, 3 * CHUNK), bf16),
             pltpu.VMEM((chunks, 2, half, 3 * CHUNK), bf16),
             pltpu.VMEM((chunks, half, 3 * CHUNK), bf16),
             pltpu.VMEM((chunks, 2, half, 3 * CHUNK), bf16),
-            pltpu.VMEM((2, 2, half, 3 * CHUNK), f32),
-            pltpu.VMEM((width, tokens), f32),
+            pltpu.VMEM((4, 2, half, 3 * CHUNK), f32),
             pltpu.VMEM((tokens, width), f32),
             pltpu.VMEM((4, rows, width), f32),
-            pltpu.VMEM((3, rows, width), bf16),
-            pltpu.VMEM((3, rows, width), bf16),
             dma((3, chunks)), dma((2, 7)), dma((2, 7)),
             dma((chunks, 2)), dma((chunks, 2)), dma((chunks,)), dma((chunks,)),
             dma((3, chunks)), dma((chunks, 2)),
-            dma((4,)), dma((4,)), dma((3,)), dma((3,)), dma((2,)),
+            dma((4,)), dma((4,)), dma((2,)),
         ],
         compiler_params=pltpu.CompilerParams(
             collective_id=0, has_side_effects=True, vmem_limit_bytes=56 * 1024 * 1024
@@ -429,11 +418,14 @@
 
 
 def on_device_fused(activations, out_grad, w_gate, w_up, w_down):
-    in_grad, act_t, grad, hidden_t, gate_grad, up_grad = exchange(
+    own, *terms, act_t, grad, hidden_t, gate_grad, up_grad = exchange(
         activations, out_grad, w_gate, w_up, w_down
     )
+    for flip, term in zip((2, 4, 6), terms):
+        term = lax.ppermute(term, "row", [(i, i ^ flip) for i in range(8)])
+        own += term.astype(jnp.float32)
     grad_gate, grad_up, grad_down = outer_products(act_t, grad, hidden_t, gate_grad, up_grad)
-    return (in_grad, grad_gate, grad_up, grad_down)
+    return (own.astype(jnp.bfloat16), grad_gate, grad_up, grad_down)
 
 
 def solution(mesh):

time: 83 us -> 76.4 us (0.920)
  Pallas kernels: 80.5 us -> 71 us
  starting transfers between devices: 0 us -> 3.55 us
    pallas_call x1, Pallas kernels: 70.2 us -> 60.7 us  [exchange(): pl.pallas_call(exchange_kernel, out_shape=(jax.ShapeDtypeStruct((rows, wi...]
    ppermute x0 -> x3, starting transfers between devices: none -> 3.55 us  [on_device_fused(): term = lax.ppermute(term, 'row', [(i, i ^ flip) for i in range(8)])]
  transfers between devices with their start and end apart: 0 -> 3, of which waited for: 0 -> 0; matrix products, arithmetic and copies ran while one was open for 0% -> 0% of each run, Pallas kernels for 0% -> 14%
where the time goes in v3:
time: 76.4 us; the launch traced here: 75.9 us
  Pallas kernels  71 us (93%)
  starting transfers between devices  3.55 us (5%)
    pallas_call x1, Pallas kernels, exchange(): pl.pallas_call(exchange_kernel, out_shape=(jax.ShapeDtypeStruct((rows, wi...  60.7 us
    pallas_call x1, Pallas kernels, outer_products(): pl.pallas_call(outer_kernel, grid=(steps,), out_shape=(jax.ShapeDtypeStru...  10.3 us
    ppermute x3, starting transfers between devices, on_device_fused(): term = lax.ppermute(term, 'row', [(i, i ^ flip) for i in range(8)])  3.55 us
  transfers between devices with their start and end apart: 3, of which 0 were waited for; matrix products, arithmetic and copies ran while one was open for 0% of the time, Pallas kernels for 14%

profile of v3, /device:TPU:0, one launch (start us, length us, event | category | flops | bytes accessed | tf_op | source)
XLA Modules:
  0.0 75.9 jit_solution(13141222339604715153)
XLA Ops:
  0.6 60.7 %shard_map.84 = (f32[16,2048]{1,0:T(8,128)}, bf16[16,2048]{1,0:T(8,128)(2,1)}, bf16[16,2048]{1,0:T(8,128)(2,1)}, bf16[16,2048]{1,0:T(8,128)(2,1)}, bf16[2048,128...) custom-call(bf16[16,2048]{1,0:T(8,128)(2,1)} %act_ref.1, ...), custom_call_target="tpu_custom_call" | custom-call | flops 4697620480 | bytes 22020096 | tf_op jit(solution)/shard_map/pallas_call | solution.py:329
  61.3 0.0 copy-start
  61.4 1.2 %collective-permute-start = (bf16[16,2048]{1,0:T(8,128)(2,1)}, bf16[16,2048]{1,0:T(8,128)(2,1)S(1)}, u32[]{:S(2)}, u32[]{:S(2)}) collective-permute-start(bf16[16,2048]{1,0:T(8,128)(2,1)} %get-tuple-element.17), channel_id=1, source_target_pairs={{0,8},{4,12},{8,0},{12,4},{16,24},{20,28},{24,16},{28,20},{1,9},{5... | collective-permute-start | bytes 196616 | tf_op jit(solution)/shard_map/ppermute | solution.py:425
  62.6 1.7 %collective-permute-start.1 = (bf16[16,2048]{1,0:T(8,128)(2,1)}, bf16[16,2048]{1,0:T(8,128)(2,1)S(1)}, u32[]{:S(2)}, u32[]{:S(2)}) collective-permute-start(bf16[16,2048]{1,0:T(8,128)(2,1)} %get-tuple-element.18), channel_id=1, source_target_pairs={{0,16},{4,20},{8,24},{12,28},{16,0},{20,4},{24,8},{28,12},{1,17},{... | collective-permute-start | bytes 196616 | tf_op jit(solution)/shard_map/ppermute | solution.py:425
  64.3 0.6 collective-permute-start.2
  64.9 10.3 %shard_map.85 = (bf16[2048,1792]{1,0:T(8,128)(2,1)}, bf16[2048,1792]{1,0:T(8,128)(2,1)}, bf16[1792,2048]{1,0:T(8,128)(2,1)}) custom-call(bf16[2048,128]{1,0:T(8,128)(2,1)} %get-tuple-element.20.act_t_ref, bf16[128,2048]{1,0:T(8,128)(2,1)} %get-tuple-element.21.grad_ref, bf16[1792,128]{1,0:T(8,128)(2,1)} %get-tuple-element.22.hidden_t_ref, ...), custom_call_target="tpu_custom_call" | custom-call | flops 2818572288 | bytes 22020096 | tf_op jit(solution)/shard_map/pallas_call | solution.py:391
  75.2 0.0 collective-permute-done
  75.2 0.0 collective-permute-done.1
  75.2 0.0 collective-permute-done.2
  75.2 0.0 copy-done
  75.2 0.7 add_convert_fusion
Async XLA Ops:
  61.3 13.9 %copy-start = (f32[16,2048]{1,0:T(8,128)S(1)}, f32[16,2048]{1,0:T(8,128)}, u32[]{:S(2)}) copy-start(f32[16,2048]{1,0:T(8,128)} %get-tuple-element.16) | copy-start | bytes 393220
  61.4 13.9 %collective-permute-start = (bf16[16,2048]{1,0:T(8,128)(2,1)}, bf16[16,2048]{1,0:T(8,128)(2,1)S(1)}, u32[]{:S(2)}, u32[]{:S(2)}) collective-permute-start(bf16[16,2048]{1,0:T(8,128)(2,1)} %get-tuple-element.17), channel_id=1, source_target_pairs={{0,8},{4,12},{8,0},{12,4},{16,24},{20,28},{24,16},{28,20},{1,9},{5... | collective-permute-start | bytes 196616 | tf_op jit(solution)/shard_map/ppermute | solution.py:425
  62.6 12.7 %collective-permute-start.1 = (bf16[16,2048]{1,0:T(8,128)(2,1)}, bf16[16,2048]{1,0:T(8,128)(2,1)S(1)}, u32[]{:S(2)}, u32[]{:S(2)}) collective-permute-start(bf16[16,2048]{1,0:T(8,128)(2,1)} %get-tuple-element.18), channel_id=1, source_target_pairs={{0,16},{4,20},{8,24},{12,28},{16,0},{20,4},{24,8},{28,12},{1,17},{... | collective-permute-start | bytes 196616 | tf_op jit(solution)/shard_map/ppermute | solution.py:425
  64.3 11.0 %collective-permute-start.2 = (bf16[16,2048]{1,0:T(8,128)(2,1)}, bf16[16,2048]{1,0:T(8,128)(2,1)S(1)}, u32[]{:S(2)}, u32[]{:S(2)}) collective-permute-start(bf16[16,2048]{1,0:T(8,128)(2,1)} %get-tuple-element.19), channel_id=1, source_target_pairs={{0,24},{4,28},{8,16},{12,20},{16,8},{20,12},{24,0},{28,4},{1,25},{... | collective-permute-start | bytes 196616 | tf_op jit(solution)/shard_map/ppermute | solution.py:425

commit v4 on v3

--- a/solution.py
+++ b/solution.py
@@ -66,10 +66,11 @@
 
 def exchange_kernel(
     act_ref, grad_ref, wg_ref, wu_ref, wd_ref,
-    mine_ref, x_ref, y_ref, diag_ref, act_t_out, grad_out, hidden_t_out, gate_out, up_out,
+    mine_ref, x_ref, y_ref, diag_ref, act_t_hbm, grad_hbm, hidden_t_hbm, gate_hbm, up_hbm,
     both, wgu, wdn, ep, rp, xp, res, own, acc, pair,
     w_sem, gat_send, gat_recv, ep_send, rp_recv, xp_send, xp_recv, res_send, res_recv,
-    pair_send, pair_recv, own_sem,
+    pair_send, pair_recv, own_sem, out_sem,
+    act_t_out, hidden_t_out, gate_out, up_out,
 ):
     chip_refs = (x_ref, y_ref, diag_ref)
     chunks = wgu.shape[0]
@@ -136,13 +137,11 @@
 
     def gather(a, index, to, kind):
         return pltpu.make_async_remote_copy(
-            src_ref=block(a, index), dst_ref=block(a, index),
+            src_ref=(act_ref, grad_ref)[a] if index is r else block(a, index), dst_ref=block(a, index),
             send_sem=gat_send.at[a, kind], recv_sem=gat_recv.at[a, kind],
             device_id=(to, c), device_id_type=MESH,
         )
 
-    for copy in locals_:
-        copy.wait()
     sent = []
     for a in (0, 1):
         sent += [gather(a, r, xn, 0), gather(a, r, yn, 1), gather(a, r, sib, 3)]
@@ -170,6 +169,11 @@
         for kind, index in ((3, r), (4, xn), (5, yn), (6, dg)):
             gather(a, index + sib - r, sib, kind).wait_recv()
 
+    for copy in locals_:
+        copy.wait()
+    grad_copy = pltpu.make_async_copy(both.at[1], grad_hbm, out_sem.at[0])
+    grad_copy.start()
+
     inner = jnp.where(c == 0, 1, 2)
     outer = jnp.where(c == 1, 0, 3)
     peer = 3 - c
@@ -222,7 +226,6 @@
         def _():
             span = pl.ds(pl.multiple_of(j * (width // 8), width // 8), width // 8)
             act_t_out[span, :] = both[0, :, span].T
-            grad_out[:, span] = both[1, :, span]
 
     @pl.when(end)
     def _():
@@ -291,8 +294,12 @@
         lax.fori_loop(0, chunks + PASS_LAG, step, 0)
         lax.fori_loop(0, chunks, drain, 0)
 
-    for copy in sent:
-        copy.wait_send()
+    outs = [grad_copy] + [
+        pltpu.make_async_copy(src, dst, out_sem.at[k + 1])
+        for k, (src, dst) in enumerate(
+            ((act_t_out, act_t_hbm), (hidden_t_out, hidden_t_hbm), (gate_out, gate_hbm), (up_out, up_hbm))
+        )
+    ]
 
     def term(index):
         return pl.ds(pl.multiple_of(index * rows, rows), rows)
@@ -306,6 +313,10 @@
 
     for k in range(4):
         to_sib(k).start()
+    for copy in outs[1:]:
+        copy.start()
+    for copy in sent:
+        copy.wait_send()
     for k in range(4):
         to_sib(k).wait_recv()
 
@@ -317,6 +328,8 @@
         chip_refs[kind][...] = summed(to).astype(jnp.bfloat16)
     for k in range(4):
         to_sib(k).wait_send()
+    for copy in outs:
+        copy.wait()
 
 
 def exchange(activations, out_grad, w_gate, w_up, w_down):
@@ -340,7 +353,7 @@
             jax.ShapeDtypeStruct((tokens, hidden), bf16),
         ),
         in_specs=[vmem, vmem, anywhere, anywhere, anywhere],
-        out_specs=(vmem,) * 9,
+        out_specs=(vmem,) * 4 + (anywhere,) * 5,
         scratch_shapes=[
             pltpu.VMEM((2, tokens, width), bf16),
             pltpu.VMEM((chunks, width, 2 * CHUNK), bf16),
@@ -355,7 +368,11 @@
             dma((3, chunks)), dma((2, 7)), dma((2, 7)),
             dma((chunks, 2)), dma((chunks, 2)), dma((chunks,)), dma((chunks,)),
             dma((3, chunks)), dma((chunks, 2)),
-            dma((4,)), dma((4,)), dma((2,)),
+            dma((4,)), dma((4,)), dma((2,)), dma((5,)),
+            pltpu.VMEM((width, tokens), bf16),
+            pltpu.VMEM((hidden, tokens), bf16),
+            pltpu.VMEM((tokens, hidden), bf16),
+            pltpu.VMEM((tokens, hidden), bf16),
         ],
         compiler_params=pltpu.CompilerParams(
             collective_id=0, has_side_effects=True, vmem_limit_bytes=56 * 1024 * 1024

time: 76.4 us -> 75.6 us (0.990)
  Pallas kernels: 71 us -> 70.2 us
    pallas_call x1, Pallas kernels: 60.7 us -> 59.9 us  [exchange(): pl.pallas_call(exchange_kernel, out_shape=(jax.ShapeDtypeStruct((rows, wi...]
where the time goes in v4:
time: 75.6 us; the launch traced here: 75.1 us
  Pallas kernels  70.2 us (93%)
  starting transfers between devices  3.55 us (5%)
    pallas_call x1, Pallas kernels, exchange(): pl.pallas_call(exchange_kernel, out_shape=(jax.ShapeDtypeStruct((rows, wi...  59.9 us
    pallas_call x1, Pallas kernels, outer_products(): pl.pallas_call(outer_kernel, grid=(steps,), out_shape=(jax.ShapeDtypeStru...  10.3 us
    ppermute x3, starting transfers between devices, on_device_fused(): term = lax.ppermute(term, 'row', [(i, i ^ flip) for i in range(8)])  3.55 us
  transfers between devices with their start and end apart: 3, of which 0 were waited for; matrix products, arithmetic and copies ran while one was open for 0% of the time, Pallas kernels for 14%

profile of v4, /device:TPU:0, one launch (start us, length us, event | category | flops | bytes accessed | tf_op | source)
XLA Modules:
  0.0 75.1 jit_solution(5242675386328489059)
XLA Ops:
  0.6 59.9 %shard_map.84 = (f32[16,2048]{1,0:T(8,128)}, bf16[16,2048]{1,0:T(8,128)(2,1)}, bf16[16,2048]{1,0:T(8,128)(2,1)}, bf16[16,2048]{1,0:T(8,128)(2,1)}, bf16[2048,128...) custom-call(bf16[16,2048]{1,0:T(8,128)(2,1)} %act_ref.1, ...), custom_call_target="tpu_custom_call" | custom-call | flops 4697620480 | bytes 22020096 | tf_op jit(solution)/shard_map/pallas_call | solution.py:342
  60.6 0.0 copy-start
  60.6 1.2 %collective-permute-start = (bf16[16,2048]{1,0:T(8,128)(2,1)}, bf16[16,2048]{1,0:T(8,128)(2,1)S(1)}, u32[]{:S(2)}, u32[]{:S(2)}) collective-permute-start(bf16[16,2048]{1,0:T(8,128)(2,1)} %get-tuple-element.17), channel_id=1, source_target_pairs={{0,8},{4,12},{8,0},{12,4},{16,24},{20,28},{24,16},{28,20},{1,9},{5... | collective-permute-start | bytes 196616 | tf_op jit(solution)/shard_map/ppermute | solution.py:442
  61.8 1.7 %collective-permute-start.1 = (bf16[16,2048]{1,0:T(8,128)(2,1)}, bf16[16,2048]{1,0:T(8,128)(2,1)S(1)}, u32[]{:S(2)}, u32[]{:S(2)}) collective-permute-start(bf16[16,2048]{1,0:T(8,128)(2,1)} %get-tuple-element.18), channel_id=1, source_target_pairs={{0,16},{4,20},{8,24},{12,28},{16,0},{20,4},{24,8},{28,12},{1,17},{... | collective-permute-start | bytes 196616 | tf_op jit(solution)/shard_map/ppermute | solution.py:442
  63.5 0.6 collective-permute-start.2
  64.1 10.3 %shard_map.85 = (bf16[2048,1792]{1,0:T(8,128)(2,1)}, bf16[2048,1792]{1,0:T(8,128)(2,1)}, bf16[1792,2048]{1,0:T(8,128)(2,1)}) custom-call(bf16[2048,128]{1,0:T(8,128)(2,1)} %get-tuple-element.20.act_t_ref, bf16[128,2048]{1,0:T(8,128)(2,1)} %get-tuple-element.21.grad_ref, bf16[1792,128]{1,0:T(8,128)(2,1)} %get-tuple-element.22.hidden_t_ref, ...), custom_call_target="tpu_custom_call" | custom-call | flops 2818572288 | bytes 22020096 | tf_op jit(solution)/shard_map/pallas_call | solution.py:408
  74.4 0.0 collective-permute-done
  74.4 0.0 collective-permute-done.1
  74.5 0.0 collective-permute-done.2
  74.5 0.0 copy-done
  74.5 0.7 add_convert_fusion
Async XLA Ops:
  60.6 13.9 %copy-start = (f32[16,2048]{1,0:T(8,128)S(1)}, f32[16,2048]{1,0:T(8,128)}, u32[]{:S(2)}) copy-start(f32[16,2048]{1,0:T(8,128)} %get-tuple-element.16) | copy-start | bytes 393220
  60.6 13.9 %collective-permute-start = (bf16[16,2048]{1,0:T(8,128)(2,1)}, bf16[16,2048]{1,0:T(8,128)(2,1)S(1)}, u32[]{:S(2)}, u32[]{:S(2)}) collective-permute-start(bf16[16,2048]{1,0:T(8,128)(2,1)} %get-tuple-element.17), channel_id=1, source_target_pairs={{0,8},{4,12},{8,0},{12,4},{16,24},{20,28},{24,16},{28,20},{1,9},{5... | collective-permute-start | bytes 196616 | tf_op jit(solution)/shard_map/ppermute | solution.py:442
  61.8 12.6 %collective-permute-start.1 = (bf16[16,2048]{1,0:T(8,128)(2,1)}, bf16[16,2048]{1,0:T(8,128)(2,1)S(1)}, u32[]{:S(2)}, u32[]{:S(2)}) collective-permute-start(bf16[16,2048]{1,0:T(8,128)(2,1)} %get-tuple-element.18), channel_id=1, source_target_pairs={{0,16},{4,20},{8,24},{12,28},{16,0},{20,4},{24,8},{28,12},{1,17},{... | collective-permute-start | bytes 196616 | tf_op jit(solution)/shard_map/ppermute | solution.py:442
  63.5 11.0 %collective-permute-start.2 = (bf16[16,2048]{1,0:T(8,128)(2,1)}, bf16[16,2048]{1,0:T(8,128)(2,1)S(1)}, u32[]{:S(2)}, u32[]{:S(2)}) collective-permute-start(bf16[16,2048]{1,0:T(8,128)(2,1)} %get-tuple-element.19), channel_id=1, source_target_pairs={{0,24},{4,28},{8,16},{12,20},{16,8},{20,12},{24,0},{28,4},{1,25},{... | collective-permute-start | bytes 196616 | tf_op jit(solution)/shard_map/ppermute | solution.py:442

commit v5 on v4

--- a/solution.py
+++ b/solution.py
@@ -53,7 +53,7 @@
 
 MESH = pl.DeviceIdType.MESH
 CHUNK = 128
-ADD_LAG, PASS_LAG = 2, 4
+ADD_LAG, PASS_LAG = 3, 6
 
 
 def nt_dot(a, b):

time: 75.6 us -> 78.7 us (1.041)
  Pallas kernels: 70.2 us -> 73.3 us
    pallas_call x1, Pallas kernels: 59.9 us -> 63 us  [exchange(): pl.pallas_call(exchange_kernel, out_shape=(jax.ShapeDtypeStruct((rows, wi...]
  transfers between devices with their start and end apart: 3 -> 3, of which waited for: 0 -> 0; matrix products, arithmetic and copies ran while one was open for 0% -> 0% of each run, Pallas kernels for 14% -> 13%
where the time goes in v5:
time: 78.7 us; the launch traced here: 78.2 us
  Pallas kernels  73.3 us (93%)
  starting transfers between devices  3.56 us (5%)
    pallas_call x1, Pallas kernels, exchange(): pl.pallas_call(exchange_kernel, out_shape=(jax.ShapeDtypeStruct((rows, wi...  63 us
    pallas_call x1, Pallas kernels, outer_products(): pl.pallas_call(outer_kernel, grid=(steps,), out_shape=(jax.ShapeDtypeStru...  10.3 us
    ppermute x3, starting transfers between devices, on_device_fused(): term = lax.ppermute(term, 'row', [(i, i ^ flip) for i in range(8)])  3.56 us
  transfers between devices with their start and end apart: 3, of which 0 were waited for; matrix products, arithmetic and copies ran while one was open for 0% of the time, Pallas kernels for 13%

profile of v5, /device:TPU:0, one launch (start us, length us, event | category | flops | bytes accessed | tf_op | source)
XLA Modules:
  0.0 78.2 jit_solution(8170024980867098396)
XLA Ops:
  0.6 63.0 %shard_map.84 = (f32[16,2048]{1,0:T(8,128)}, bf16[16,2048]{1,0:T(8,128)(2,1)}, bf16[16,2048]{1,0:T(8,128)(2,1)}, bf16[16,2048]{1,0:T(8,128)(2,1)}, bf16[2048,128...) custom-call(bf16[16,2048]{1,0:T(8,128)(2,1)} %act_ref.1, ...), custom_call_target="tpu_custom_call" | custom-call | flops 4697620480 | bytes 22020096 | tf_op jit(solution)/shard_map/pallas_call | solution.py:342
  63.6 0.0 copy-start
  63.7 0.1 collective-permute-start
  63.7 1.9 %collective-permute-start.1 = (bf16[16,2048]{1,0:T(8,128)(2,1)}, bf16[16,2048]{1,0:T(8,128)(2,1)S(1)}, u32[]{:S(2)}, u32[]{:S(2)}) collective-permute-start(bf16[16,2048]{1,0:T(8,128)(2,1)} %get-tuple-element.18), channel_id=1, source_target_pairs={{0,16},{4,20},{8,24},{12,28},{16,0},{20,4},{24,8},{28,12},{1,17},{... | collective-permute-start | bytes 196616 | tf_op jit(solution)/shard_map/ppermute | solution.py:442
  65.6 1.6 %collective-permute-start.2 = (bf16[16,2048]{1,0:T(8,128)(2,1)}, bf16[16,2048]{1,0:T(8,128)(2,1)S(1)}, u32[]{:S(2)}, u32[]{:S(2)}) collective-permute-start(bf16[16,2048]{1,0:T(8,128)(2,1)} %get-tuple-element.19), channel_id=1, source_target_pairs={{0,24},{4,28},{8,16},{12,20},{16,8},{20,12},{24,0},{28,4},{1,25},{... | collective-permute-start | bytes 196616 | tf_op jit(solution)/shard_map/ppermute | solution.py:442
  67.2 10.3 %shard_map.85 = (bf16[2048,1792]{1,0:T(8,128)(2,1)}, bf16[2048,1792]{1,0:T(8,128)(2,1)}, bf16[1792,2048]{1,0:T(8,128)(2,1)}) custom-call(bf16[2048,128]{1,0:T(8,128)(2,1)} %get-tuple-element.20.act_t_ref, bf16[128,2048]{1,0:T(8,128)(2,1)} %get-tuple-element.21.grad_ref, bf16[1792,128]{1,0:T(8,128)(2,1)} %get-tuple-element.22.hidden_t_ref, ...), custom_call_target="tpu_custom_call" | custom-call | flops 2818572288 | bytes 22020096 | tf_op jit(solution)/shard_map/pallas_call | solution.py:408
  77.5 0.0 collective-permute-done
  77.5 0.0 collective-permute-done.1
  77.5 0.0 collective-permute-done.2
  77.6 0.0 copy-done
  77.6 0.7 add_convert_fusion
Async XLA Ops:
  63.6 13.9 %copy-start = (f32[16,2048]{1,0:T(8,128)S(1)}, f32[16,2048]{1,0:T(8,128)}, u32[]{:S(2)}) copy-start(f32[16,2048]{1,0:T(8,128)} %get-tuple-element.16) | copy-start | bytes 393220
  63.7 13.9 %collective-permute-start = (bf16[16,2048]{1,0:T(8,128)(2,1)}, bf16[16,2048]{1,0:T(8,128)(2,1)S(1)}, u32[]{:S(2)}, u32[]{:S(2)}) collective-permute-start(bf16[16,2048]{1,0:T(8,128)(2,1)} %get-tuple-element.17), channel_id=1, source_target_pairs={{0,8},{4,12},{8,0},{12,4},{16,24},{20,28},{24,16},{28,20},{1,9},{5... | collective-permute-start | bytes 196616 | tf_op jit(solution)/shard_map/ppermute | solution.py:442
  63.7 13.8 %collective-permute-start.1 = (bf16[16,2048]{1,0:T(8,128)(2,1)}, bf16[16,2048]{1,0:T(8,128)(2,1)S(1)}, u32[]{:S(2)}, u32[]{:S(2)}) collective-permute-start(bf16[16,2048]{1,0:T(8,128)(2,1)} %get-tuple-element.18), channel_id=1, source_target_pairs={{0,16},{4,20},{8,24},{12,28},{16,0},{20,4},{24,8},{28,12},{1,17},{... | collective-permute-start | bytes 196616 | tf_op jit(solution)/shard_map/ppermute | solution.py:442
  65.6 11.9 %collective-permute-start.2 = (bf16[16,2048]{1,0:T(8,128)(2,1)}, bf16[16,2048]{1,0:T(8,128)(2,1)S(1)}, u32[]{:S(2)}, u32[]{:S(2)}) collective-permute-start(bf16[16,2048]{1,0:T(8,128)(2,1)} %get-tuple-element.19), channel_id=1, source_target_pairs={{0,24},{4,28},{8,16},{12,20},{16,8},{20,12},{24,0},{28,4},{1,25},{... | collective-permute-start | bytes 196616 | tf_op jit(solution)/shard_map/ppermute | solution.py:442
